TPU v7x, 32 devices: a whole 2x2x4 slice. The times are simulated.
32 devices in a mesh: dp: 8 (over z, y), fsdp: 4 (over x, core).
Axes of the slice: x: 2, y: 2, z: 4, core: 2. Of those that a mesh axis runs over, the one named last changes fastest.
Arguments:
- hidden: bfloat16 [32, 256, 1152], P(('dp', 'fsdp')), may hold values from -6 to 6
- attn_out: bfloat16 [32, 256, 1152], P(('dp', 'fsdp')), may hold values from -6 to 6
- proj_weight: bfloat16 [1152, 1152], P('fsdp'), may hold values from -0.1875 to 0.1875
- norm_gain: float32 [1152], replicated, may hold values from 0.1 to 1.9
- norm_bias: float32 [1152], replicated, may hold values from -3 to 3
- feature_cot: bfloat16 [8, 1024, 1152], P('dp', 'fsdp'), may hold values from -6 to 6
Outputs:
- features: bfloat16 [8, 1024, 1152], P('dp', 'fsdp')
- grad_hidden: bfloat16 [32, 256, 1152], P(('dp', 'fsdp'))
- grad_attn: bfloat16 [32, 256, 1152], P(('dp', 'fsdp'))
- grad_weight: bfloat16 [1152, 1152], P('fsdp')
All inputs are finite; a program needn't handle non-finite values.
Results may differ from a plain program's by a relative error of at most 0.018.
Values may be sent and summed in bfloat16 or wider, within the bound.
A program may use at most 64 MiB of HBM per device.

v0:
```python
import math

import jax
import jax.numpy as jnp
from jax import lax
from jax.sharding import PartitionSpec as P


def local(hidden, attn_out, proj_weight, norm_gain, norm_bias, feature_cot):
    images, patches, width = hidden.shape
    groups = lax.axis_size("fsdp")
    total = images * patches * lax.axis_size("dp") * groups
    factor = 1.0 / math.sqrt(total)
    rows = images * patches
    attn_rows = attn_out.reshape(rows, width)
    full_weight = lax.all_gather(proj_weight, "fsdp", axis=0, tiled=True)
    projected = jnp.dot(attn_rows, full_weight, preferred_element_type=jnp.float32)
    stream = hidden.reshape(rows, width).astype(jnp.float32) + projected
    mean_rows = jnp.mean(stream, axis=-1, keepdims=True)
    centered = stream - mean_rows
    variance = jnp.mean(centered * centered, axis=-1, keepdims=True)
    inverse = lax.rsqrt(variance + 1e-06)
    normed = centered * inverse
    local_features = (
        (normed * norm_gain + norm_bias).astype(jnp.bfloat16).reshape(images, patches, width)
    )
    moved = lax.all_to_all(local_features, "fsdp", split_axis=1, concat_axis=0, tiled=True)
    features = moved.reshape(1, rows, width)
    incoming = feature_cot.reshape(images * groups, patches // groups, width)
    returned = lax.all_to_all(incoming, "fsdp", split_axis=0, concat_axis=1, tiled=True)
    scaled = returned.reshape(rows, width).astype(jnp.float32) * norm_gain
    grad_stream = inverse * (
        scaled
        - jnp.mean(scaled, axis=-1, keepdims=True)
        - normed * jnp.mean(scaled * normed, axis=-1, keepdims=True)
    )
    grad_hidden = grad_stream.astype(jnp.bfloat16)
    grad_attn = lax.dot_general(
        grad_hidden, full_weight, (((1,), (1,)), ((), ())), preferred_element_type=jnp.float32
    ).astype(jnp.bfloat16)
    product = lax.dot_general(
        attn_rows, grad_hidden, (((0,), (0,)), ((), ())), preferred_element_type=jnp.float32
    )
    partial_rows = lax.psum_scatter(
        (product * factor).astype(jnp.bfloat16), "fsdp", scatter_dimension=0, tiled=True
    ).astype(jnp.float32)
    grad_weight = lax.psum(partial_rows, "dp").astype(jnp.bfloat16)
    return (
        features,
        grad_hidden.reshape(images, patches, width),
        grad_attn.reshape(images, patches, width),
        grad_weight,
    )


def solution(mesh):
    return jax.shard_map(
        local,
        mesh=mesh,
        in_specs=(
            P(("dp", "fsdp"), None, None),
            P(("dp", "fsdp"), None, None),
            P("fsdp", None),
            P(),
            P(),
            P("dp", "fsdp", None),
        ),
        out_specs=(
            P("dp", "fsdp", None),
            P(("dp", "fsdp"), None, None),
            P(("dp", "fsdp"), None, None),
            P("fsdp", None),
        ),
        check_vma=False,
    )
```

profile of v0, /device:TPU:0, one launch (start us, length us, event | category | flops | bytes accessed | tf_op | source)
XLA Modules:
  0.0 172.3 jit_solution(7409484372325024365)
XLA Ops:
  7.2 0.0 copy-start
  7.2 0.0 copy-start.4
  7.2 0.0 copy-start.6
  7.2 0.0 all-gather.2.cloned.1.call-start
  7.2 0.7 all-gather.2.cloned.1.call-update
  7.9 0.0 reduce-scatter.4.cloned.1.call-start
  8.0 13.8 %all_to_all.8 = bf16[4,64,1152]{2,1,0:T(8,128)(2,1)S(1)} all-to-all(bf16[4,64,1152]{2,1,0:T(8,128)(2,1)} %bitcast.35), channel_id=1, replica_groups=mesh['dp'=8,'fsdp'=4] {'fsdp'}, dimensions={0} | all-to-all | bytes 1179648 | tf_op jit(solution)/shard_map/all_to_all | solution.py:30
  21.8 0.0 copy-done.4
  21.8 0.2 multiply_reduce_fusion.1
  22.0 0.1 div.17
  22.0 16.0 %all-gather.2.cloned.1.call-done = bf16[1152,1152]{1,0:T(8,128)(2,1)} async-done(((bf16[288,1152]{1,0:T(8,128)(2,1)}), bf16[1152,1152]{1,0:T(8,128)(2,1)}) %all-gather.2.cloned.1.call-update) | async-done | bytes 2654224 | tf_op jit(solution)/shard_map/all_gather | solution.py:16
  38.1 0.0 copy-done
  38.1 0.0 copy-done.6
  38.1 2.8 %fusion.6 = (f32[256]{0:T(256)S(1)}, f32[256,1152]{1,0:T(8,128)S(1)}) fusion(bf16[1152,1152]{1,0:T(8,128)(2,1)} %all-gather.2.cloned.1.call-done, bf16[1,256,1152]{2,1,0:T(8,128)(2,1)S(1)} %copy-done, bf16[1,256,1152]{2,1,0:T(8,128)(2,1)S(1)} %copy-done.6), kind=kOutput, calls=%fused_computation.20 | convolution fusion | flops 680361728 | bytes 5014528 | tf_op jit(solution)/shard_map/dot_general | solution.py:17
  40.9 0.3 multiply_reduce_fusion.2
  41.2 0.0 copy-start.5
  41.2 0.4 multiply_reduce_fusion
  41.6 0.3 copy-done.5
  41.9 1.3 multiply_convert_fusion
  43.2 0.0 copy-start.2
  43.2 0.8 copy-done.2
  44.0 1.0 fusion.1
  45.0 3.3 %copy.14 = bf16[1152,1152]{1,0:T(8,128)(2,1)} copy(bf16[1152,1152]{0,1:T(8,128)(2,1)S(1)} %fusion.1) | data formatting | bytes 5308416
  48.3 0.0 reduce-scatter.4.cloned.1.call-update
  48.3 0.0 copy-start.1
  48.3 0.0 all-reduce.2.cloned.1.call-start
  48.4 35.4 %reduce-scatter.4.cloned.1.call-done = bf16[288,1152]{1,0:T(8,128)(2,1)} async-done(((bf16[1152,1152]{1,0:T(8,128)(2,1)}), bf16[288,1152]{1,0:T(8,128)(2,1)}) %reduce-scatter.4.cloned.1.call-update) | async-done | bytes 663568
  83.8 2.3 %copy.15 = bf16[288,1152]{0,1:T(8,128)(2,1)} copy(bf16[288,1152]{1,0:T(8,128)(2,1)} %reduce-scatter.4.cloned.1.call-done) | data formatting | bytes 1327104
  86.1 0.0 all-reduce.2.cloned.1.call-update
  86.1 0.0 copy-done.1
  86.1 0.9 copy.17
  87.1 0.5 broadcast.52
  87.6 4.2 %reduce.4 = bf16[256,1152]{1,0:T(8,128)(2,1)S(1)} reduce(bf16[256,1,1152]{2,1,0:T(2,128)(2,1)S(1)} %bitcast.33, bf16[]{:T(256)} %broadcast.52), dimensions={1}, to_apply=%bitcast.32.reduce_sub_computation | reduce | bytes 1179650
  91.8 0.0 copy-start.3
  91.8 1.0 reshape.84
  92.8 3.5 %all-to-all-start = ((bf16[4,2,36864]{2,1,0:T(2,128)(2,1)}), bf16[4,2,36864]{2,1,0:T(2,128)(2,1)S(1)}, u32[]{:S(2)}, u32[]{:S(2)}) async-start(bf16[4,2,36864]{2,1,0:T(2,128)(2,1)} %reshape.84), calls=%async_computation | async-start | bytes 1179648 | tf_op jit(solution)/shard_map/all_to_all | solution.py:27
  96.3 0.0 copy-done.3
  96.3 3.6 %fusion.2 = bf16[1,256,1152]{2,1,0:T(8,128)(2,1)} fusion(bf16[256,1152]{1,0:T(8,128)(2,1)S(1)} %copy-done.3, bf16[1152,1152]{1,0:T(8,128)(2,1)} %all-gather.2.cloned.1.call-done), kind=kOutput, calls=%fused_computation.5 | convolution fusion | flops 679772160 | bytes 3833856 | tf_op jit(solution)/shard_map/dot_general | solution.py:38
  99.9 5.9 %all-to-all-done = bf16[4,2,36864]{2,1,0:T(2,128)(2,1)S(1)} async-done(((bf16[4,2,36864]{2,1,0:T(2,128)(2,1)}), bf16[4,2,36864]{2,1,0:T(2,128)(2,1)S(1)}, u32[]{:S(2)}, u32[]{:S(2)}) %all-to-all-start) | async-done | bytes 589856 | tf_op jit(solution)/shard_map/all_to_all | solution.py:27
  105.8 0.6 reshape.85
  106.4 0.9 copy.12
  107.2 56.3 %all-reduce.2.cloned.1.call-done = bf16[288,1152]{0,1:T(8,128)(2,1)} async-done(((bf16[288,1152]{0,1:T(8,128)(2,1)}), bf16[288,1152]{0,1:T(8,128)(2,1)}) %all-reduce.2.cloned.1.call-update) | async-done | bytes 663568 | tf_op jit(solution)/shard_map/psum | solution.py:47
  163.5 2.3 %copy.13 = bf16[288,1152]{1,0:T(8,128)(2,1)} copy(bf16[288,1152]{0,1:T(8,128)(2,1)} %all-reduce.2.cloned.1.call-done) | data formatting | bytes 1327104
  (4 shorter events, 0.0 us)
Async XLA Ops:
  7.2 30.9 %copy-start = (bf16[1,256,1152]{2,1,0:T(8,128)(2,1)S(1)}, bf16[1,256,1152]{2,1,0:T(8,128)(2,1)}, u32[]{:S(2)}) copy-start(bf16[1,256,1152]{2,1,0:T(8,128)(2,1)} %param.7) | copy-start | bytes 1769476
  7.2 14.6 %copy-start.4 = (f32[1152]{0:T(1024)S(1)}, f32[1152]{0:T(1024)}, u32[]{:S(2)}) copy-start(f32[1152]{0:T(1024)} %param.9) | copy-start | bytes 13828
  7.2 30.9 %copy-start.6 = (bf16[1,256,1152]{2,1,0:T(8,128)(2,1)S(1)}, bf16[1,256,1152]{2,1,0:T(8,128)(2,1)}, u32[]{:S(2)}) copy-start(bf16[1,256,1152]{2,1,0:T(8,128)(2,1)} %param.6) | copy-start | bytes 1769476
  7.2 30.9 %all-gather.2.cloned.1.call-start = ((), (), s32[]{:S(2)}) async-start(), calls=%async_computation.3 | async-start | bytes 3317760 | tf_op jit(solution)/shard_map/all_gather | solution.py:16
  7.9 75.8 %reduce-scatter.4.cloned.1.call-start = ((), (), s32[]{:S(2)}) async-start(), calls=%async_computation.5 | async-start | bytes 3317760
  41.2 0.7 copy-start.5
  43.2 0.8 copy-start.2
  48.3 37.8 %copy-start.1 = (bf16[1,256,1152]{2,1,0:T(8,128)(2,1)S(1)}, bf16[1,256,1152]{2,1,0:T(8,128)(2,1)}, u32[]{:S(2)}) copy-start(bf16[1,256,1152]{2,1,0:T(8,128)(2,1)} %get-tuple-element.13) | copy-start | bytes 1769476
  48.3 115.2 %all-reduce.2.cloned.1.call-start = ((), (), s32[]{:S(2)}) async-start(), calls=%async_computation.4 | async-start | bytes 1769472 | tf_op jit(solution)/shard_map/psum | solution.py:47
  91.8 4.5 %copy-start.3 = (bf16[256,1152]{1,0:T(8,128)(2,1)S(1)}, bf16[256,1152]{1,0:T(8,128)(2,1)}, u32[]{:S(2)}) copy-start(bf16[256,1152]{1,0:T(8,128)(2,1)} %copy-done.2) | copy-start | bytes 1769476
  92.8 13.0 %all-to-all-start = ((bf16[4,2,36864]{2,1,0:T(2,128)(2,1)}), bf16[4,2,36864]{2,1,0:T(2,128)(2,1)S(1)}, u32[]{:S(2)}, u32[]{:S(2)}) async-start(bf16[4,2,36864]{2,1,0:T(2,128)(2,1)} %reshape.84), calls=%async_computation | async-start | bytes 1179648 | tf_op jit(solution)/shard_map/all_to_all | solution.py:27
Sparse Core Ops, SparseCore 0:
  9.6 28.4 all-gather.1
  48.4 35.3 reduce-scatter.3
  87.6 75.8 all-reduce.1
where the time goes:
time: 173 us; the launch traced here: 172 us
  waiting for transfers between devices  114 us (66%)
  between operations  13.9 us (8%)
  blocking collectives  13.8 us (8%)
  local copies, waits for them, and re-layouts  12.9 us (7%)
  matrix products  7.42 us (4%)
  other arithmetic  6.39 us (4%)
  starting transfers between devices  3.59 us (2%)
    psum x1, waiting for transfers between devices, local(): grad_weight = lax.psum(partial_rows, 'dp').astype(jnp.bfloat16)  56.3 us
    unnamed x4, waiting for transfers between devices  36.1 us
    all_gather x1, waiting for transfers between devices, local(): full_weight = lax.all_gather(proj_weight, 'fsdp', axis=0, tiled=True)  16 us
    all_to_all x1, blocking collectives, local(): lax.all_to_all(incoming, 'fsdp', split_axis=0, concat_axis=1, tiled=True)  13.8 us
    unnamed x21, local copies, waits for them, and re-layouts  12 us
    all_to_all x1, waiting for transfers between devices, local(): lax.all_to_all(local_features, 'fsdp', split_axis=1, concat_axis=0, tiled...  5.9 us
    unnamed x1, other arithmetic  4.21 us
    dot_general x1, matrix products, local(): lax.dot_general(grad_hidden, full_weight, (((1,), (1,)), ((), ())), prefe...  3.6 us
  transfers between devices with their start and end apart: 4, of which 4 were waited for; matrix products, arithmetic and copies ran while one was open for 7% of the time, Pallas kernels for 0%

commit v1 on v0

--- a/solution.py
+++ b/solution.py
@@ -1,14 +1,385 @@
+import functools
 import math
 
 import jax
 import jax.numpy as jnp
 from jax import lax
+from jax.experimental import pallas as pl
+from jax.experimental.pallas import tpu as pltpu
 from jax.sharding import PartitionSpec as P
+
+MESH = pl.DeviceIdType.MESH
+F32 = jnp.float32
+BF16 = jnp.bfloat16
+
+
+def column_pieces(width):
+    tiles = width // 128
+    return next(count for count in (3, 2, 1) if tiles % count == 0)
+
+
+def semaphores(pieces):
+    return 14 + 6 * pieces
+
+
+def kernel(
+    n, ndp, factor,
+    hidden_h, attn_h, weight_h, gain, bias, cot_h,
+    features_h, gh_h, ga_h, gw_h,
+    hid, att, att_t, peer_t, weight, cot, proj, feat, gh, gh_peer, ga,
+    far, near, x_send, x_recv, y_keep, y_send, y_recv, z_own, z_up, z_mid, gw,
+    send_sem, recv_sem, local_sem,
+):
+    rows, width = att.shape
+    shard = weight_h.shape[0]
+    half = shard // 2
+    block = rows // n
+    pieces = column_pieces(width)
+    span = width // pieces
+    chain = ndp // 2
+    d = lax.axis_index("dp")
+    f = lax.axis_index("fsdp")
+    core = f + 1 - 2 * (f % 2)
+    across = (f + n // 2) % n
+    diagonal = (core + n // 2) % n
+    peers = (core, across, diagonal)
+    bit = d % 2
+    side = d + 1 - 2 * bit
+    z = d // 2
+    low = z < chain // 2
+    step = jnp.where(low, 2, -2)
+    inner = d + step
+    outer = d - step
+    outermost = (z == 0) | (z == chain - 1)
+    middle = (z == chain // 2 - 1) | (z == chain // 2)
+
+    def remote(src, dst, index, dev):
+        return pltpu.make_async_remote_copy(
+            src_ref=src, dst_ref=dst, send_sem=send_sem.at[index],
+            recv_sem=recv_sem.at[index], device_id=dev, device_id_type=MESH,
+        )
+
+    def local(src, dst, index):
+        return pltpu.make_async_copy(src, dst, local_sem.at[index])
+
+    def rows_of(start, size, align):
+        return pl.ds(pl.multiple_of(start, align), size)
+
+    def shard_rows(owner):
+        return rows_of(owner * shard, shard, 16)
+
+    def half_rows(owner, which):
+        return rows_of(owner * shard + which * half, half, 16)
+
+    def block_rows(which):
+        return rows_of(which * block, block, 16)
+
+    load_att = local(attn_h, att, 0)
+    load_weight = local(weight_h, weight.at[shard_rows(f)], 1)
+    load_hid = local(hidden_h, hid, 2)
+    load_cot = local(cot_h.at[block_rows(f)], cot.at[block_rows(f)], 3)
+    loads = (load_att, load_weight, load_hid, load_cot)
+    for copy in loads:
+        copy.start()
+
+    barrier = pltpu.get_barrier_semaphore()
+    for peer in peers:
+        pl.semaphore_signal(barrier, inc=1, device_id=(d, peer), device_id_type=MESH)
+    pl.semaphore_signal(barrier, inc=1, device_id=(side, f), device_id_type=MESH)
+    pl.semaphore_signal(barrier, inc=1, device_id=(inner, f), device_id_type=MESH)
+
+    @pl.when(jnp.logical_not(outermost))
+    def _():
+        pl.semaphore_signal(barrier, inc=1, device_id=(outer, f), device_id_type=MESH)
+        pl.semaphore_wait(barrier, len(peers) + 3)
+
+    @pl.when(outermost)
+    def _():
+        pl.semaphore_wait(barrier, len(peers) + 2)
+
+    sent = []
+
+    def go(src, dst, index, dev):
+        copy = remote(src, dst, index, dev)
+        copy.start()
+        sent.append(copy)
+
+    def arrived(dst, index, dev):
+        remote(dst, dst, index, dev).wait_recv()
+
+    go(weight_h.at[rows_of(bit * half, half, 16)], weight.at[half_rows(f, bit)], 1, (d, across))
+    go(weight_h, weight.at[shard_rows(f)], 0, (d, core))
+    for k, peer in ((2, across), (3, diagonal), (1, core)):
+        go(cot_h.at[block_rows(peer)], cot.at[block_rows(f)], 4 + k, (d, peer))
+
+    load_att.wait()
+    for start in range(0, width, 128):
+        att_t[start:start + 128, :] = att[:, start:start + 128].T
+    go(att_t.at[shard_rows(core)], peer_t.at[0], 8, (d, core))
+    go(att_t.at[shard_rows(diagonal)], peer_t.at[1], 9, (d, core))
+
+    first = weight.at[half_rows(across, bit)]
+    arrived(first, 1, (d, across))
+    go(first, first, 2, (side, f))
+    go(first, first, 3, (d, core))
+    second = weight.at[half_rows(across, 1 - bit)]
+    arrived(second, 2, (side, f))
+    go(second, second, 4, (d, core))
+    load_weight.wait()
+    load_hid.wait()
+    arrived(weight.at[shard_rows(core)], 0, (d, core))
+    arrived(weight.at[half_rows(diagonal, bit)], 3, (d, core))
+    arrived(weight.at[half_rows(diagonal, 1 - bit)], 4, (d, core))
+
+    for p in range(pieces):
+        cols = slice(p * span, (p + 1) * span)
+        proj[:, cols] = jnp.dot(att[...], weight[:, cols], preferred_element_type=F32)
+
+    load_cot.wait()
+    for k, peer in ((1, core), (2, across), (3, diagonal)):
+        arrived(cot.at[block_rows(peer)], 4 + k, (d, peer))
+
+    strip = 16
+
+    def norm(index, carry):
+        at = rows_of(index * strip, strip, strip)
+        stream = hid[at, :].astype(F32) + proj[at, :]
+        centered = stream - jnp.mean(stream, axis=-1, keepdims=True)
+        variance = jnp.mean(centered * centered, axis=-1, keepdims=True)
+        inverse = lax.rsqrt(variance + 1e-06)
+        normed = centered * inverse
+        feat[at, :] = (normed * gain[...] + bias[...]).astype(BF16)
+        scaled = cot[at, :].astype(F32) * gain[...]
+        grad = inverse * (
+            scaled
+            - jnp.mean(scaled, axis=-1, keepdims=True)
+            - normed * jnp.mean(scaled * normed, axis=-1, keepdims=True)
+        )
+        gh[at, :] = grad.astype(BF16)
+        return carry
+
+    lax.fori_loop(0, rows // strip, norm, 0)
+
+    go(gh, gh_peer, 10, (d, core))
+    go(feat.at[block_rows(core)], features_h.at[block_rows(f)], 11, (d, core))
+    store_feat = local(feat.at[block_rows(f)], features_h.at[block_rows(f)], 0)
+    store_gh = local(gh, gh_h, 1)
+    store_feat.start()
+    store_gh.start()
+
+    def own_term(owner, cols):
+        return jnp.dot(att_t[shard_rows(owner), :], gh[:, cols], preferred_element_type=F32)
+
+    def peer_term(slot, cols):
+        return jnp.dot(peer_t[slot], gh_peer[:, cols], preferred_element_type=F32)
+
+    spans = [slice(p * span, (p + 1) * span) for p in range(pieces)]
+    for p in range(pieces):
+        far[p] = own_term(across, spans[p])
+    arrived(peer_t.at[0], 8, (d, core))
+    arrived(peer_t.at[1], 9, (d, core))
+    arrived(gh_peer, 10, (d, core))
+    base = 14
+    for p in range(pieces):
+        x_send[p] = ((far[p] + peer_term(1, spans[p])) * factor).astype(BF16)
+        go(x_send.at[p], x_recv.at[p], base + p, (d, across))
+    for k, peer in ((2, across), (3, diagonal)):
+        go(feat.at[block_rows(peer)], features_h.at[block_rows(f)], 10 + k, (d, peer))
+    for p in range(pieces):
+        near[p] = (own_term(f, spans[p]) + peer_term(0, spans[p])) * factor
+    for p in range(pieces):
+        ga[:, spans[p]] = lax.dot_general(
+            gh[...], weight[spans[p], :], (((1,), (1,)), ((), ())), preferred_element_type=F32
+        ).astype(BF16)
+    store_ga = local(ga, ga_h, 2)
+    store_ga.start()
+
+    own_half = rows_of(bit * half, half, 16)
+    other_half = rows_of((1 - bit) * half, half, 16)
+
+    def result(p):
+        return gw.at[own_half, spans[p]]
+
+    def up(p):
+        return remote(z_own.at[p], z_up.at[p], base + 2 * pieces + p, (inner, f))
+
+    def mid(p):
+        return remote(z_own.at[p], z_mid.at[p], base + 3 * pieces + p, (inner, f))
+
+    def down(p):
+        return remote(result(p), result(p), base + 4 * pieces + p, (outer, f))
+
+    def gather(p):
+        return remote(result(p), result(p), base + 5 * pieces + p, (side, f))
+
+    def stage_x(p):
+        arrived(x_recv.at[p], base + p, (d, across))
+        y_send[p] = (near[p, other_half, :] + x_recv[p, other_half, :].astype(F32)).astype(BF16)
+        go(y_send.at[p], y_recv.at[p], base + pieces + p, (side, f))
+        y_keep[p] = near[p, own_half, :] + x_recv[p, own_half, :].astype(F32)
+
+    def stage_y(p):
+        arrived(y_recv.at[p], base + pieces + p, (side, f))
+
+        @pl.when(outermost)
+        def _():
+            z_own[p] = (y_keep[p] + y_recv[p].astype(F32)).astype(BF16)
+
+            @pl.when(jnp.logical_not(middle))
+            def _():
+                up(p).start()
+
+            @pl.when(middle)
+            def _():
+                mid(p).start()
+
+    def stage_up(p):
+        @pl.when(jnp.logical_not(outermost))
+        def _():
+            up(p).wait_recv()
+            total = y_keep[p] + y_recv[p].astype(F32) + z_up[p].astype(F32)
+            z_own[p] = total.astype(BF16)
+
+            @pl.when(jnp.logical_not(middle))
+            def _():
+                up(p).start()
+
+            @pl.when(middle)
+            def _():
+                mid(p).start()
+
+    def stage_mid(p):
+        @pl.when(middle)
+        def _():
+            mid(p).wait_recv()
+            total = z_own[p].astype(F32) + z_mid[p].astype(F32)
+            gw[own_half, spans[p]] = total.astype(BF16)
+            gather(p).start()
+
+            @pl.when(jnp.logical_not(outermost))
+            def _():
+                down(p).start()
+
+    def stage_down(p):
+        @pl.when(jnp.logical_not(middle))
+        def _():
+            down(p).wait_recv()
+            gather(p).start()
+
+            @pl.when(jnp.logical_not(outermost))
+            def _():
+                down(p).start()
+
+    def stage_gather(p):
+        there = gw.at[other_half, spans[p]]
+        arrived(there, base + 5 * pieces + p, (side, f))
+
+    stages = (stage_x, stage_y, stage_up, stage_mid, stage_down, stage_gather)
+    for turn in range(pieces + len(stages) - 1):
+        for depth in reversed(range(len(stages))):
+            if 0 <= turn - depth < pieces:
+                stages[depth](turn - depth)
+
+    store_gw = local(gw, gw_h, 3)
+    store_gw.start()
+    for copy in sent:
+        copy.wait_send()
+    for p in range(pieces):
+        gather(p).wait_send()
+
+        @pl.when(middle)
+        def _():
+            mid(p).wait_send()
+
+        @pl.when(jnp.logical_not(middle))
+        def _():
+            up(p).wait_send()
+
+        @pl.when(jnp.logical_not(outermost))
+        def _():
+            down(p).wait_send()
+
+    for k, peer in ((1, core), (2, across), (3, diagonal)):
+        arrived(features_h.at[block_rows(peer)], 10 + k, (d, peer))
+    for copy in (store_feat, store_gh, store_ga, store_gw):
+        copy.wait()
+
+
+def fused(hidden, attn_out, proj_weight, norm_gain, norm_bias, feature_cot):
+    images, patches, width = hidden.shape
+    n = lax.axis_size("fsdp")
+    ndp = lax.axis_size("dp")
+    rows = images * patches
+    shard = proj_weight.shape[0]
+    factor = 1.0 / math.sqrt(rows * n * ndp)
+    pieces = column_pieces(width)
+    span = width // pieces
+    half = shard // 2
+    vmem = pltpu.VMEM
+    any_spec = pl.BlockSpec(memory_space=pl.ANY)
+    vmem_spec = pl.BlockSpec(memory_space=vmem)
+    matrix = jax.ShapeDtypeStruct((rows, width), BF16)
+    outs = pl.pallas_call(
+        functools.partial(kernel, n, ndp, factor),
+        out_shape=(matrix, matrix, matrix, jax.ShapeDtypeStruct((shard, width), BF16)),
+        in_specs=[any_spec, any_spec, any_spec, vmem_spec, vmem_spec, any_spec],
+        out_specs=(any_spec,) * 4,
+        scratch_shapes=[
+            vmem((rows, width), BF16),
+            vmem((rows, width), BF16),
+            vmem((width, rows), BF16),
+            vmem((2, shard, rows), BF16),
+            vmem((width, width), BF16),
+            vmem((rows, width), BF16),
+            vmem((rows, width), F32),
+            vmem((rows, width), BF16),
+            vmem((rows, width), BF16),
+            vmem((rows, width), BF16),
+            vmem((rows, width), BF16),
+            vmem((pieces, shard, span), F32),
+            vmem((pieces, shard, span), F32),
+            vmem((pieces, shard, span), BF16),
+            vmem((pieces, shard, span), BF16),
+            vmem((pieces, half, span), F32),
+            vmem((pieces, half, span), BF16),
+            vmem((pieces, half, span), BF16),
+            vmem((pieces, half, span), BF16),
+            vmem((pieces, half, span), BF16),
+            vmem((pieces, half, span), BF16),
+            vmem((shard, width), BF16),
+            pltpu.SemaphoreType.DMA((semaphores(pieces),)),
+            pltpu.SemaphoreType.DMA((semaphores(pieces),)),
+            pltpu.SemaphoreType.DMA((4,)),
+        ],
+        compiler_params=pltpu.CompilerParams(
+            collective_id=0, has_side_effects=True, vmem_limit_bytes=40 * 1024 * 1024
+        ),
+        cost_estimate=pl.CostEstimate(
+            flops=6 * rows * width * width, bytes_accessed=16 * rows * width, transcendentals=rows
+        ),
+    )(
+        hidden.reshape(rows, width), attn_out.reshape(rows, width), proj_weight,
+        norm_gain.reshape(1, width), norm_bias.reshape(1, width),
+        feature_cot.reshape(rows, width),
+    )
+    shape = (images, patches, width)
+    features, grad_hidden, grad_attn, grad_weight = outs
+    return (
+        features.reshape(1, rows, width), grad_hidden.reshape(shape),
+        grad_attn.reshape(shape), grad_weight,
+    )
 
 
 def local(hidden, attn_out, proj_weight, norm_gain, norm_bias, feature_cot):
     images, patches, width = hidden.shape
     groups = lax.axis_size("fsdp")
+    shard = proj_weight.shape[0]
+    planned = (
+        groups == 2 * 2 and lax.axis_size("dp") % 4 == 0 and images == 1
+        and shard % 32 == 0 and width % 128 == 0 and patches % (16 * groups) == 0
+    )
+    if planned:
+        return fused(hidden, attn_out, proj_weight, norm_gain, norm_bias, feature_cot)
     total = images * patches * lax.axis_size("dp") * groups
     factor = 1.0 / math.sqrt(total)
     rows = images * patches

time: 173 us -> 78.9 us (0.46)
  waiting for transfers between devices: 114 us -> 0 us
  Pallas kernels: 0 us -> 69.6 us
  blocking collectives: 13.8 us -> 0 us
  between operations: 13.9 us -> 0.66 us
  matrix products: 7.42 us -> 0 us
  other arithmetic: 6.39 us -> 0 us
  local copies, waits for them, and re-layouts: 12.9 us -> 8.28 us
  starting transfers between devices: 3.59 us -> 0 us
    pallas_call x0 -> x1, Pallas kernels: none -> 69.6 us  [fused(): pl.pallas_call(functools.partial(kernel, n, ndp, factor), out_shape=(matr...]
    psum x1 -> x0, waiting for transfers between devices: 56.3 us -> none  [local(): grad_weight = lax.psum(partial_rows, 'dp').astype(jnp.bfloat16)]
    unnamed x4 -> x0, waiting for transfers between devices: 36.1 us -> none
    all_gather x1 -> x0, waiting for transfers between devices: 16 us -> none  [local(): full_weight = lax.all_gather(proj_weight, 'fsdp', axis=0, tiled=True)]
    all_to_all x1 -> x0, blocking collectives: 13.8 us -> none  [local(): lax.all_to_all(incoming, 'fsdp', split_axis=0, concat_axis=1, tiled=True)]
    dot_general x3 -> x0, matrix products: 7.42 us -> none  [the longest x1 3.6 us: local(): lax.dot_general(grad_hidden, full_weight, (((1,), (1,)), ((), ())), prefe...]
    all_to_all x1 -> x0, waiting for transfers between devices: 5.9 us -> none  [local(): lax.all_to_all(local_features, 'fsdp', split_axis=1, concat_axis=0, tiled...]
    unnamed x21 -> x14, local copies, waits for them, and re-layouts: 12 us -> 7.56 us
  transfers between devices with their start and end apart: 4 -> 0, of which waited for: 4 -> 0; matrix products, arithmetic and copies ran while one was open for 7% -> 0% of each run, Pallas kernels for 0% -> 0%
where the time goes in v1:
time: 78.9 us; the launch traced here: 78.6 us
  Pallas kernels  69.6 us (88%)
  local copies, waits for them, and re-layouts  8.28 us (10%)
    pallas_call x1, Pallas kernels, fused(): pl.pallas_call(functools.partial(kernel, n, ndp, factor), out_shape=(matr...  69.6 us
    unnamed x14, local copies, waits for them, and re-layouts  7.56 us

profile of v1, /device:TPU:0, one launch (start us, length us, event | category | flops | bytes accessed | tf_op | source)
XLA Modules:
  0.0 78.6 jit_solution(454032894331822778)
XLA Ops:
  0.6 0.0 copy-start.4
  0.6 0.7 reshape.34.gain
  1.3 0.0 copy-done.4
  1.4 0.0 copy-start
  1.4 1.1 %copy-done = bf16[288,1152]{1,0:T(8,128)(2,1)S(1)} copy-done((bf16[288,1152]{1,0:T(8,128)(2,1)S(1)}, bf16[288,1152]{1,0:T(8,128)(2,1)}, u32[]{:S(2)}) %copy-start) | copy-done | bytes 663576
  2.5 0.0 copy-start.1
  2.5 1.1 %copy-done.1 = bf16[1,256,1152]{2,1,0:T(8,128)(2,1)S(1)} copy-done((bf16[1,256,1152]{2,1,0:T(8,128)(2,1)S(1)}, bf16[1,256,1152]{2,1,0:T(8,128)(2,1)}, u32[]{:S(2)}) %copy-start.1) | copy-done | bytes 589848
  3.5 0.0 copy-start.2
  3.5 1.1 %copy-done.2 = bf16[1,256,1152]{2,1,0:T(8,128)(2,1)S(1)} copy-done((bf16[1,256,1152]{2,1,0:T(8,128)(2,1)S(1)}, bf16[1,256,1152]{2,1,0:T(8,128)(2,1)}, u32[]{:S(2)}) %copy-start.2) | copy-done | bytes 589848
  4.6 0.0 copy-start.3
  4.6 1.1 %copy-done.3 = bf16[1,256,1152]{2,1,0:T(8,128)(2,1)S(1)} copy-done((bf16[1,256,1152]{2,1,0:T(8,128)(2,1)S(1)}, bf16[1,256,1152]{2,1,0:T(8,128)(2,1)}, u32[]{:S(2)}) %copy-start.3) | copy-done | bytes 589848
  5.6 69.6 %shard_map.93 = (bf16[256,1152]{1,0:T(8,128)(2,1)S(1)}, bf16[256,1152]{1,0:T(8,128)(2,1)S(1)}, bf16[256,1152]{1,0:T(8,128)(2,1)S(1)}, bf16[288,1152]{1,0:T(8,128)(2,1)S(1)}) custom-call(bf16[256,1152]{1,0:T(8,128)(2,1)S(1)} %bitcast.9, bf16[256,1152]{1,0:T(8,128)(2,1)S(1)} %bitcast.10, bf16[288,1152]{1,0:T(8,128)(2,1)S(1)} %copy-done, ...), custom_call_target="tpu_custom_call" | custom-call | flops 2038431744 | bytes 4718592 | tf_op jit(solution)/shard_map/pallas_call | solution.py:322
  75.3 0.8 %copy.14 = bf16[1,256,1152]{2,1,0:T(8,128)(2,1)} copy(bf16[1,256,1152]{2,1,0:T(8,128)(2,1)S(1)} %bitcast.8) | data formatting | bytes 1179648
  76.1 0.8 %copy.15 = bf16[1,256,1152]{2,1,0:T(8,128)(2,1)} copy(bf16[1,256,1152]{2,1,0:T(8,128)(2,1)S(1)} %bitcast.7) | data formatting | bytes 1179648
  76.9 0.8 %copy.16 = bf16[1,256,1152]{2,1,0:T(8,128)(2,1)} copy(bf16[1,256,1152]{2,1,0:T(8,128)(2,1)S(1)} %bitcast.6) | data formatting | bytes 1179648
  77.7 0.8 %copy.17 = bf16[288,1152]{1,0:T(8,128)(2,1)} copy(bf16[288,1152]{1,0:T(8,128)(2,1)S(1)} %get-tuple-element.19) | data formatting | bytes 1327104
  (1 shorter events, 0.0 us)
Async XLA Ops:
  0.6 0.7 copy-start.4
  1.4 1.1 %copy-start = (bf16[288,1152]{1,0:T(8,128)(2,1)S(1)}, bf16[288,1152]{1,0:T(8,128)(2,1)}, u32[]{:S(2)}) copy-start(bf16[288,1152]{1,0:T(8,128)(2,1)} %weight_h.1) | copy-start | bytes 1990660
  2.5 1.1 %copy-start.1 = (bf16[1,256,1152]{2,1,0:T(8,128)(2,1)S(1)}, bf16[1,256,1152]{2,1,0:T(8,128)(2,1)}, u32[]{:S(2)}) copy-start(bf16[1,256,1152]{2,1,0:T(8,128)(2,1)} %param.6) | copy-start | bytes 1769476
  3.5 1.1 %copy-start.2 = (bf16[1,256,1152]{2,1,0:T(8,128)(2,1)S(1)}, bf16[1,256,1152]{2,1,0:T(8,128)(2,1)}, u32[]{:S(2)}) copy-start(bf16[1,256,1152]{2,1,0:T(8,128)(2,1)} %param.7) | copy-start | bytes 1769476
  4.6 1.1 %copy-start.3 = (bf16[1,256,1152]{2,1,0:T(8,128)(2,1)S(1)}, bf16[1,256,1152]{2,1,0:T(8,128)(2,1)}, u32[]{:S(2)}) copy-start(bf16[1,256,1152]{2,1,0:T(8,128)(2,1)} %param.11) | copy-start | bytes 1769476

commit v2 on v1

--- a/solution.py
+++ b/solution.py
@@ -18,8 +18,12 @@
     return next(count for count in (3, 2, 1) if tiles % count == 0)
 
 
-def semaphores(pieces):
-    return 14 + 6 * pieces
+def part_count(half):
+    return next(count for count in (3, 2, 1) if half % (16 * count) == 0)
+
+
+def semaphores(pieces, parts):
+    return 14 + 6 * pieces + 4 * parts
 
 
 def kernel(
@@ -68,8 +72,11 @@
     def shard_rows(owner):
         return rows_of(owner * shard, shard, 16)
 
-    def half_rows(owner, which):
-        return rows_of(owner * shard + which * half, half, 16)
+    parts = part_count(half)
+    part = half // parts
+
+    def part_rows(owner, which, index):
+        return rows_of(owner * shard + which * half + index * part, part, 16)
 
     def block_rows(which):
         return rows_of(which * block, block, 16)
@@ -98,6 +105,7 @@
         pl.semaphore_wait(barrier, len(peers) + 2)
 
     sent = []
+    wbase = 14 + 6 * pieces
 
     def go(src, dst, index, dev):
         copy = remote(src, dst, index, dev)
@@ -107,10 +115,11 @@
     def arrived(dst, index, dev):
         remote(dst, dst, index, dev).wait_recv()
 
-    go(weight_h.at[rows_of(bit * half, half, 16)], weight.at[half_rows(f, bit)], 1, (d, across))
+    for i in range(parts):
+        source = weight_h.at[rows_of(bit * half + i * part, part, 16)]
+        go(source, weight.at[part_rows(f, bit, i)], wbase + i, (d, across))
     go(weight_h, weight.at[shard_rows(f)], 0, (d, core))
-    for k, peer in ((2, across), (3, diagonal), (1, core)):
-        go(cot_h.at[block_rows(peer)], cot.at[block_rows(f)], 4 + k, (d, peer))
+    go(cot_h.at[block_rows(core)], cot.at[block_rows(f)], 5, (d, core))
 
     load_att.wait()
     for start in range(0, width, 128):
@@ -118,18 +127,24 @@
     go(att_t.at[shard_rows(core)], peer_t.at[0], 8, (d, core))
     go(att_t.at[shard_rows(diagonal)], peer_t.at[1], 9, (d, core))
 
-    first = weight.at[half_rows(across, bit)]
-    arrived(first, 1, (d, across))
-    go(first, first, 2, (side, f))
-    go(first, first, 3, (d, core))
-    second = weight.at[half_rows(across, 1 - bit)]
-    arrived(second, 2, (side, f))
-    go(second, second, 4, (d, core))
+    for i in range(parts):
+        first = weight.at[part_rows(across, bit, i)]
+        arrived(first, wbase + i, (d, across))
+        go(first, first, wbase + parts + i, (side, f))
+        go(first, first, wbase + 2 * parts + i, (d, core))
+    for k, peer in ((2, across), (3, diagonal)):
+        go(cot_h.at[block_rows(peer)], cot.at[block_rows(f)], 4 + k, (d, peer))
+    for i in range(parts):
+        second = weight.at[part_rows(across, 1 - bit, i)]
+        arrived(second, wbase + parts + i, (side, f))
+        go(second, second, wbase + 3 * parts + i, (d, core))
     load_weight.wait()
     load_hid.wait()
     arrived(weight.at[shard_rows(core)], 0, (d, core))
-    arrived(weight.at[half_rows(diagonal, bit)], 3, (d, core))
-    arrived(weight.at[half_rows(diagonal, 1 - bit)], 4, (d, core))
+    for i in range(parts):
+        arrived(weight.at[part_rows(diagonal, bit, i)], wbase + 2 * parts + i, (d, core))
+    for i in range(parts):
+        arrived(weight.at[part_rows(diagonal, 1 - bit, i)], wbase + 3 * parts + i, (d, core))
 
     for p in range(pieces):
         cols = slice(p * span, (p + 1) * span)
@@ -162,6 +177,7 @@
 
     go(gh, gh_peer, 10, (d, core))
     go(feat.at[block_rows(core)], features_h.at[block_rows(f)], 11, (d, core))
+    go(feat.at[block_rows(across)], features_h.at[block_rows(f)], 12, (d, across))
     store_feat = local(feat.at[block_rows(f)], features_h.at[block_rows(f)], 0)
     store_gh = local(gh, gh_h, 1)
     store_feat.start()
@@ -183,8 +199,6 @@
     for p in range(pieces):
         x_send[p] = ((far[p] + peer_term(1, spans[p])) * factor).astype(BF16)
         go(x_send.at[p], x_recv.at[p], base + p, (d, across))
-    for k, peer in ((2, across), (3, diagonal)):
-        go(feat.at[block_rows(peer)], features_h.at[block_rows(f)], 10 + k, (d, peer))
     for p in range(pieces):
         near[p] = (own_term(f, spans[p]) + peer_term(0, spans[p])) * factor
     for p in range(pieces):
@@ -217,6 +231,8 @@
         y_send[p] = (near[p, other_half, :] + x_recv[p, other_half, :].astype(F32)).astype(BF16)
         go(y_send.at[p], y_recv.at[p], base + pieces + p, (side, f))
         y_keep[p] = near[p, own_half, :] + x_recv[p, own_half, :].astype(F32)
+        if p == pieces - 1:
+            go(feat.at[block_rows(diagonal)], features_h.at[block_rows(f)], 13, (d, diagonal))
 
     def stage_y(p):
         arrived(y_recv.at[p], base + pieces + p, (side, f))
@@ -317,12 +333,13 @@
     half = shard // 2
     vmem = pltpu.VMEM
     any_spec = pl.BlockSpec(memory_space=pl.ANY)
+    hbm_spec = pl.BlockSpec(memory_space=pltpu.HBM)
     vmem_spec = pl.BlockSpec(memory_space=vmem)
     matrix = jax.ShapeDtypeStruct((rows, width), BF16)
     outs = pl.pallas_call(
         functools.partial(kernel, n, ndp, factor),
         out_shape=(matrix, matrix, matrix, jax.ShapeDtypeStruct((shard, width), BF16)),
-        in_specs=[any_spec, any_spec, any_spec, vmem_spec, vmem_spec, any_spec],
+        in_specs=[hbm_spec, hbm_spec, hbm_spec, vmem_spec, vmem_spec, hbm_spec],
         out_specs=(any_spec,) * 4,
         scratch_shapes=[
             vmem((rows, width), BF16),
@@ -347,12 +364,12 @@
             vmem((pieces, half, span), BF16),
             vmem((pieces, half, span), BF16),
             vmem((shard, width), BF16),
-            pltpu.SemaphoreType.DMA((semaphores(pieces),)),
-            pltpu.SemaphoreType.DMA((semaphores(pieces),)),
+            pltpu.SemaphoreType.DMA((semaphores(pieces, part_count(half)),)),
+            pltpu.SemaphoreType.DMA((semaphores(pieces, part_count(half)),)),
             pltpu.SemaphoreType.DMA((4,)),
         ],
         compiler_params=pltpu.CompilerParams(
-            collective_id=0, has_side_effects=True, vmem_limit_bytes=40 * 1024 * 1024
+            collective_id=0, has_side_effects=True, vmem_limit_bytes=60 * 1024 * 1024
         ),
         cost_estimate=pl.CostEstimate(
             flops=6 * rows * width * width, bytes_accessed=16 * rows * width, transcendentals=rows

time: 78.9 us -> 75.1 us (0.952)
  Pallas kernels: 69.6 us -> 66.8 us
  local copies, waits for them, and re-layouts: 8.28 us -> 7.3 us
    pallas_call x1, Pallas kernels: 69.6 us -> 66.8 us  [fused(): pl.pallas_call(functools.partial(kernel, n, ndp, factor), out_shape=(matr...]
    unnamed x14 -> x12, local copies, waits for them, and re-layouts: 7.56 us -> 5.41 us
where the time goes in v2:
time: 75.1 us; the launch traced here: 74.8 us
  Pallas kernels  66.8 us (89%)
  local copies, waits for them, and re-layouts  7.3 us (10%)
    pallas_call x1, Pallas kernels, fused(): pl.pallas_call(functools.partial(kernel, n, ndp, factor), out_shape=(matr...  66.8 us
    unnamed x12, local copies, waits for them, and re-layouts  5.41 us

profile of v2, /device:TPU:0, one launch (start us, length us, event | category | flops | bytes accessed | tf_op | source)
XLA Modules:
  0.0 74.8 jit_solution(8869575410029848330)
XLA Ops:
  0.6 0.0 copy-start.3
  0.6 1.3 %reshape.34.gain = f32[1,1152]{1,0:T(1,128)} reshape(f32[1152]{0:T(1024)} %param.9) | data formatting | bytes 9216 | tf_op jit(solution)/shard_map/reshape | solution.py:379
  1.9 0.0 copy-done.3
  1.9 0.6 reshape.35.bias
  2.5 66.8 %shard_map.93 = (bf16[256,1152]{1,0:T(8,128)(2,1)}, bf16[256,1152]{1,0:T(8,128)(2,1)}, bf16[256,1152]{1,0:T(8,128)(2,1)}, bf16[288,1152]{1,0:T(8,128)(2,1)}) custom-call(bf16[256,1152]{1,0:T(8,128)(2,1)} %bitcast.9, bf16[256,1152]{1,0:T(8,128)(2,1)} %bitcast.10, bf16[288,1152]{1,0:T(8,128)(2,1)} %weight_h.1, f32[1,1152]{1,0:T(1,128)} %reshape.34.gain, ...), custom_call_target="tpu_custom_call" | custom-call | flops 2038431744 | bytes 4718592 | tf_op jit(solution)/shard_map/pallas_call | solution.py:339
  69.4 0.0 copy-start.2
  69.4 2.0 %copy.14 = bf16[1,256,1152]{2,1,0:T(8,128)(2,1)} copy(bf16[1,256,1152]{2,1,0:T(8,128)(2,1)} %bitcast.8) | data formatting | bytes 1179648
  71.4 0.0 copy-done.2
  71.4 0.0 copy-start.1
  71.4 0.8 %copy.15 = bf16[1,256,1152]{2,1,0:T(8,128)(2,1)} copy(bf16[1,256,1152]{2,1,0:T(8,128)(2,1)S(1)} %bitcast.7) | data formatting | bytes 1179648
  72.2 0.5 copy-done.1
  72.6 0.0 copy-start
  72.7 0.8 %copy.16 = bf16[1,256,1152]{2,1,0:T(8,128)(2,1)} copy(bf16[1,256,1152]{2,1,0:T(8,128)(2,1)S(1)} %bitcast.6) | data formatting | bytes 1179648
  73.5 0.5 copy-done
  74.0 0.8 %copy.17 = bf16[288,1152]{1,0:T(8,128)(2,1)} copy(bf16[288,1152]{1,0:T(8,128)(2,1)S(1)} %copy-done) | data formatting | bytes 1327104
Async XLA Ops:
  0.6 1.3 %copy-start.3 = (f32[1152]{0:T(1024)S(1)}, f32[1152]{0:T(1024)}, u32[]{:S(2)}) copy-start(f32[1152]{0:T(1024)} %param.10) | copy-start | bytes 13828
  69.4 2.0 %copy-start.2 = (bf16[256,1152]{1,0:T(8,128)(2,1)S(1)}, bf16[256,1152]{1,0:T(8,128)(2,1)}, u32[]{:S(2)}) copy-start(bf16[256,1152]{1,0:T(8,128)(2,1)} %get-tuple-element.9) | copy-start | bytes 1769476
  71.4 1.3 %copy-start.1 = (bf16[256,1152]{1,0:T(8,128)(2,1)S(1)}, bf16[256,1152]{1,0:T(8,128)(2,1)}, u32[]{:S(2)}) copy-start(bf16[256,1152]{1,0:T(8,128)(2,1)} %get-tuple-element.10) | copy-start | bytes 1769476
  72.6 1.3 %copy-start = (bf16[288,1152]{1,0:T(8,128)(2,1)S(1)}, bf16[288,1152]{1,0:T(8,128)(2,1)}, u32[]{:S(2)}) copy-start(bf16[288,1152]{1,0:T(8,128)(2,1)} %get-tuple-element.19) | copy-start | bytes 1990660

commit v3 on v2

--- a/solution.py
+++ b/solution.py
@@ -13,9 +13,16 @@
 BF16 = jnp.bfloat16
 
 
-def column_pieces(width):
+def column_spans(width):
     tiles = width // 128
-    return next(count for count in (3, 2, 1) if tiles % count == 0)
+    first = (4 * tiles + 8) // 9
+    second = (3 * (tiles - first) + 4) // 5
+    spans, start = [], 0
+    for count in (first, second, tiles - first - second):
+        if count:
+            spans.append(slice(start, start + count * 128))
+            start += count * 128
+    return spans
 
 
 def part_count(half):
@@ -38,8 +45,8 @@
     shard = weight_h.shape[0]
     half = shard // 2
     block = rows // n
-    pieces = column_pieces(width)
-    span = width // pieces
+    spans = column_spans(width)
+    pieces = len(spans)
     chain = ndp // 2
     d = lax.axis_index("dp")
     f = lax.axis_index("fsdp")
@@ -147,7 +154,7 @@
         arrived(weight.at[part_rows(diagonal, 1 - bit, i)], wbase + 3 * parts + i, (d, core))
 
     for p in range(pieces):
-        cols = slice(p * span, (p + 1) * span)
+        cols = spans[p]
         proj[:, cols] = jnp.dot(att[...], weight[:, cols], preferred_element_type=F32)
 
     load_cot.wait()
@@ -189,18 +196,23 @@
     def peer_term(slot, cols):
         return jnp.dot(peer_t[slot], gh_peer[:, cols], preferred_element_type=F32)
 
-    spans = [slice(p * span, (p + 1) * span) for p in range(pieces)]
-    for p in range(pieces):
-        far[p] = own_term(across, spans[p])
+    def size(p):
+        return spans[p].stop - spans[p].start
+
+    def piece(ref, p):
+        return ref.at[p, :, 0:size(p)]
+
+    for p in range(pieces):
+        far[p, :, 0:size(p)] = own_term(across, spans[p])
     arrived(peer_t.at[0], 8, (d, core))
     arrived(peer_t.at[1], 9, (d, core))
     arrived(gh_peer, 10, (d, core))
     base = 14
     for p in range(pieces):
-        x_send[p] = ((far[p] + peer_term(1, spans[p])) * factor).astype(BF16)
-        go(x_send.at[p], x_recv.at[p], base + p, (d, across))
-    for p in range(pieces):
-        near[p] = (own_term(f, spans[p]) + peer_term(0, spans[p])) * factor
+        x_send[p, :, 0:size(p)] = ((far[p, :, 0:size(p)] + peer_term(1, spans[p])) * factor).astype(BF16)
+        go(piece(x_send, p), piece(x_recv, p), base + p, (d, across))
+    for p in range(pieces):
+        near[p, :, 0:size(p)] = (own_term(f, spans[p]) + peer_term(0, spans[p])) * factor
     for p in range(pieces):
         ga[:, spans[p]] = lax.dot_general(
             gh[...], weight[spans[p], :], (((1,), (1,)), ((), ())), preferred_element_type=F32
@@ -215,10 +227,10 @@
         return gw.at[own_half, spans[p]]
 
     def up(p):
-        return remote(z_own.at[p], z_up.at[p], base + 2 * pieces + p, (inner, f))
+        return remote(piece(z_own, p), piece(z_up, p), base + 2 * pieces + p, (inner, f))
 
     def mid(p):
-        return remote(z_own.at[p], z_mid.at[p], base + 3 * pieces + p, (inner, f))
+        return remote(piece(z_own, p), piece(z_mid, p), base + 3 * pieces + p, (inner, f))
 
     def down(p):
         return remote(result(p), result(p), base + 4 * pieces + p, (outer, f))
@@ -227,19 +239,19 @@
         return remote(result(p), result(p), base + 5 * pieces + p, (side, f))
 
     def stage_x(p):
-        arrived(x_recv.at[p], base + p, (d, across))
-        y_send[p] = (near[p, other_half, :] + x_recv[p, other_half, :].astype(F32)).astype(BF16)
-        go(y_send.at[p], y_recv.at[p], base + pieces + p, (side, f))
-        y_keep[p] = near[p, own_half, :] + x_recv[p, own_half, :].astype(F32)
+        arrived(piece(x_recv, p), base + p, (d, across))
+        y_send[p, :, 0:size(p)] = (near[p, other_half, 0:size(p)] + x_recv[p, other_half, 0:size(p)].astype(F32)).astype(BF16)
+        go(piece(y_send, p), piece(y_recv, p), base + pieces + p, (side, f))
+        y_keep[p, :, 0:size(p)] = near[p, own_half, 0:size(p)] + x_recv[p, own_half, 0:size(p)].astype(F32)
         if p == pieces - 1:
             go(feat.at[block_rows(diagonal)], features_h.at[block_rows(f)], 13, (d, diagonal))
 
     def stage_y(p):
-        arrived(y_recv.at[p], base + pieces + p, (side, f))
+        arrived(piece(y_recv, p), base + pieces + p, (side, f))
 
         @pl.when(outermost)
         def _():
-            z_own[p] = (y_keep[p] + y_recv[p].astype(F32)).astype(BF16)
+            z_own[p, :, 0:size(p)] = (y_keep[p, :, 0:size(p)] + y_recv[p, :, 0:size(p)].astype(F32)).astype(BF16)
 
             @pl.when(jnp.logical_not(middle))
             def _():
@@ -253,8 +265,8 @@
         @pl.when(jnp.logical_not(outermost))
         def _():
             up(p).wait_recv()
-            total = y_keep[p] + y_recv[p].astype(F32) + z_up[p].astype(F32)
-            z_own[p] = total.astype(BF16)
+            total = y_keep[p, :, 0:size(p)] + y_recv[p, :, 0:size(p)].astype(F32) + z_up[p, :, 0:size(p)].astype(F32)
+            z_own[p, :, 0:size(p)] = total.astype(BF16)
 
             @pl.when(jnp.logical_not(middle))
             def _():
@@ -268,7 +280,7 @@
         @pl.when(middle)
         def _():
             mid(p).wait_recv()
-            total = z_own[p].astype(F32) + z_mid[p].astype(F32)
+            total = z_own[p, :, 0:size(p)].astype(F32) + z_mid[p, :, 0:size(p)].astype(F32)
             gw[own_half, spans[p]] = total.astype(BF16)
             gather(p).start()
 
@@ -328,8 +340,9 @@
     rows = images * patches
     shard = proj_weight.shape[0]
     factor = 1.0 / math.sqrt(rows * n * ndp)
-    pieces = column_pieces(width)
-    span = width // pieces
+    spans = column_spans(width)
+    pieces = len(spans)
+    span = spans[0].stop
     half = shard // 2
     vmem = pltpu.VMEM
     any_spec = pl.BlockSpec(memory_space=pl.ANY)

time: 75.1 us -> 78.8 us (1.049)
  Pallas kernels: 66.8 us -> 70.3 us
    pallas_call x1, Pallas kernels: 66.8 us -> 70.3 us  [fused(): pl.pallas_call(functools.partial(kernel, n, ndp, factor), out_shape=(matr...]
where the time goes in v3:
time: 78.8 us; the launch traced here: 78.3 us
  Pallas kernels  70.3 us (89%)
  local copies, waits for them, and re-layouts  7.3 us (9%)
    pallas_call x1, Pallas kernels, fused(): pl.pallas_call(functools.partial(kernel, n, ndp, factor), out_shape=(matr...  70.3 us
    unnamed x12, local copies, waits for them, and re-layouts  5.41 us

profile of v3, /device:TPU:0, one launch (start us, length us, event | category | flops | bytes accessed | tf_op | source)
XLA Modules:
  0.0 78.3 jit_solution(10556799547814221359)
XLA Ops:
  0.6 0.0 copy-start.3
  0.6 1.3 %reshape.34.gain = f32[1,1152]{1,0:T(1,128)} reshape(f32[1152]{0:T(1024)} %param.9) | data formatting | bytes 9216 | tf_op jit(solution)/shard_map/reshape | solution.py:392
  1.9 0.0 copy-done.3
  1.9 0.6 reshape.35.bias
  2.5 70.3 %shard_map.93 = (bf16[256,1152]{1,0:T(8,128)(2,1)}, bf16[256,1152]{1,0:T(8,128)(2,1)}, bf16[256,1152]{1,0:T(8,128)(2,1)}, bf16[288,1152]{1,0:T(8,128)(2,1)}) custom-call(bf16[256,1152]{1,0:T(8,128)(2,1)} %bitcast.9, bf16[256,1152]{1,0:T(8,128)(2,1)} %bitcast.10, bf16[288,1152]{1,0:T(8,128)(2,1)} %weight_h.1, f32[1,1152]{1,0:T(1,128)} %reshape.34.gain, ...), custom_call_target="tpu_custom_call" | custom-call | flops 2038431744 | bytes 4718592 | tf_op jit(solution)/shard_map/pallas_call | solution.py:352
  72.8 0.0 copy-start.2
  72.9 2.0 %copy.14 = bf16[1,256,1152]{2,1,0:T(8,128)(2,1)} copy(bf16[1,256,1152]{2,1,0:T(8,128)(2,1)} %bitcast.8) | data formatting | bytes 1179648
  74.8 0.0 copy-done.2
  74.8 0.0 copy-start.1
  74.8 0.8 %copy.15 = bf16[1,256,1152]{2,1,0:T(8,128)(2,1)} copy(bf16[1,256,1152]{2,1,0:T(8,128)(2,1)S(1)} %bitcast.7) | data formatting | bytes 1179648
  75.7 0.5 copy-done.1
  76.1 0.0 copy-start
  76.1 0.8 %copy.16 = bf16[1,256,1152]{2,1,0:T(8,128)(2,1)} copy(bf16[1,256,1152]{2,1,0:T(8,128)(2,1)S(1)} %bitcast.6) | data formatting | bytes 1179648
  76.9 0.5 copy-done
  77.4 0.8 %copy.17 = bf16[288,1152]{1,0:T(8,128)(2,1)} copy(bf16[288,1152]{1,0:T(8,128)(2,1)S(1)} %copy-done) | data formatting | bytes 1327104
Async XLA Ops:
  0.6 1.3 %copy-start.3 = (f32[1152]{0:T(1024)S(1)}, f32[1152]{0:T(1024)}, u32[]{:S(2)}) copy-start(f32[1152]{0:T(1024)} %param.10) | copy-start | bytes 13828
  72.8 2.0 %copy-start.2 = (bf16[256,1152]{1,0:T(8,128)(2,1)S(1)}, bf16[256,1152]{1,0:T(8,128)(2,1)}, u32[]{:S(2)}) copy-start(bf16[256,1152]{1,0:T(8,128)(2,1)} %get-tuple-element.9) | copy-start | bytes 1769476
  74.8 1.3 %copy-start.1 = (bf16[256,1152]{1,0:T(8,128)(2,1)S(1)}, bf16[256,1152]{1,0:T(8,128)(2,1)}, u32[]{:S(2)}) copy-start(bf16[256,1152]{1,0:T(8,128)(2,1)} %get-tuple-element.10) | copy-start | bytes 1769476
  76.1 1.3 %copy-start = (bf16[288,1152]{1,0:T(8,128)(2,1)S(1)}, bf16[288,1152]{1,0:T(8,128)(2,1)}, u32[]{:S(2)}) copy-start(bf16[288,1152]{1,0:T(8,128)(2,1)} %get-tuple-element.19) | copy-start | bytes 1990660
